TPU v7x, 32 devices: a whole 2x2x4 slice. The times are simulated.
32 devices in a mesh: depth: 8 (over y, x, core), rows: 4 (over z).
Axes of the slice: x: 2, y: 2, z: 4, core: 2. Of those that a mesh axis runs over, the one named last changes fastest.
Arguments:
- volume: int32 [2, 64, 128, 1024], P(None, 'depth', 'rows'), may hold values from 0 to 255
- color_map: int32 [3, 256], replicated, may hold values from 0 to 255
- alpha_map: int32 [256], replicated, may hold values from 0 to 255
Outputs:
- image: float32 [4, 128, 1024], P(None, ('rows', 'depth'))
All inputs are finite; a program needn't handle non-finite values.
Results may differ from a plain program's by a relative error of at most 0.003.
Values may be sent and summed in bfloat16 or wider, within the bound.
No kernel may reach another device: no remote copies, remote signals or barrier semaphores. Data moves between devices by JAX's collectives and lax.ppermute only.
A program may use at most 64 MiB of HBM per device.

v0:
```python
import functools

import jax
import jax.numpy as jnp
from jax import lax
from jax.experimental import pallas as pl
from jax.experimental.pallas import tpu as pltpu
from jax.sharding import PartitionSpec as P

AMBIENT = 0.3
DIFFUSE = 0.7
LIGHT_DEPTH = 0.48 * DIFFUSE
LIGHT_ROWS = 0.6 * DIFFUSE
LIGHT_COLS = 0.64 * DIFFUSE
OPACITY = 4.0
LANES = 128
SUBLANES = 8
WHOLE = pl.BlockSpec(memory_space=pltpu.VMEM)


def parity(axis):
    return lax.axis_index(axis) % 2


def ends(axis):
    position = lax.axis_index(axis)
    return position == 0, position == lax.axis_size(axis) - 1


def edges_kernel(volume_ref, rows_near_out, rows_far_out, far_out, near_out, strip_ref, plane_ref, sems):
    _, slices, height, _ = volume_ref.shape
    odd, odd_row = parity("depth"), parity("rows")
    last_tile = height // SUBLANES - 1

    def tile(i):
        return pl.ds(pl.multiple_of(i * SUBLANES, SUBLANES), SUBLANES)

    copies = [
        pltpu.make_async_copy(volume_ref.at[0, :, tile((1 - odd_row) * last_tile)], strip_ref.at[0], sems.at[0]),
        pltpu.make_async_copy(volume_ref.at[0, :, tile(odd_row * last_tile)], strip_ref.at[1], sems.at[1]),
        pltpu.make_async_copy(volume_ref.at[0, odd * (slices - 1)], plane_ref.at[0], sems.at[2]),
        pltpu.make_async_copy(volume_ref.at[0, (1 - odd) * (slices - 1)], plane_ref.at[1], sems.at[3]),
    ]
    for copy in copies:
        copy.start()

    def narrow(values):
        return values.astype(jnp.float32).astype(jnp.bfloat16)

    copies[0].wait()
    rows_near_out[...] = narrow(jnp.where(odd_row == 1, strip_ref[0, :, 0, :], strip_ref[0, :, SUBLANES - 1, :]))
    copies[1].wait()
    rows_far_out[...] = narrow(jnp.where(odd_row == 1, strip_ref[1, :, SUBLANES - 1, :], strip_ref[1, :, 0, :]))
    copies[2].wait()
    far_out[...] = narrow(plane_ref[0])
    copies[3].wait()
    near_out[...] = narrow(plane_ref[1])


def cut_edges(volume):
    _, slices, height, columns = volume.shape
    plane = jax.ShapeDtypeStruct((height, columns), jnp.bfloat16)
    strip = jax.ShapeDtypeStruct((slices, columns), jnp.bfloat16)
    return pl.pallas_call(
        edges_kernel,
        in_specs=[pl.BlockSpec(memory_space=pl.ANY)],
        out_specs=[WHOLE] * 4,
        out_shape=[strip, strip, plane, plane],
        scratch_shapes=[
            pltpu.VMEM((2, slices, SUBLANES, columns), jnp.int32),
            pltpu.VMEM((2, height, columns), jnp.int32),
            pltpu.SemaphoreType.DMA((4,)),
        ],
    )(volume)


def pick(entries, places):
    return jnp.take_along_axis(entries, places, axis=1, mode="promise_in_bounds")


def shade(grad_depth, facing, squares):
    facing = facing + LIGHT_DEPTH * grad_depth
    squares = squares + grad_depth * grad_depth
    return AMBIENT + jnp.abs(facing) * lax.rsqrt(jnp.maximum(squares, 4.0))


def interior_kernel(
    opacity_scale, volume_ref, color_ref, alpha_ref, base_ref, face_ref, square_ref, lit_ref, grad_ref, strip_ref, held_ref
):
    _, slices, height, columns = volume_ref.shape
    tiles = height // SUBLANES
    chunks = columns // LANES
    tile = (SUBLANES, LANES)
    strip = (slices, LANES)

    packed = color_ref[0:1, :] + color_ref[1:2, :] * 256 + color_ref[2:3, :] * 65536
    color_low, color_high = packed[:, :LANES], packed[:, LANES:]
    alpha_both = alpha_ref[0:1, :LANES] + alpha_ref[0:1, LANES:] * 256

    def colors(value, tables):
        low, high = tables
        place = value & (LANES - 1)
        color = jnp.where(value < LANES, pick(low, place), pick(high, place))
        parts = (color & 255, lax.shift_right_logical(color, 8) & 255, lax.shift_right_logical(color, 16))
        return [part.astype(jnp.float32) for part in parts]

    def opacity(level, table):
        entry = pick(table, level & (LANES - 1))
        entry = lax.shift_right_logical(entry, lax.shift_right_logical(level & LANES, 4)) & 255
        return entry.astype(jnp.float32) * opacity_scale

    tile_colors = [jnp.broadcast_to(t, tile) for t in (color_low, color_high)]
    tile_alpha = jnp.broadcast_to(alpha_both, tile)
    strip_colors = [jnp.broadcast_to(t, strip) for t in (color_low, color_high)]

    def masks(shape):
        lane = lax.broadcasted_iota(jnp.int32, shape, 1)
        row = lax.broadcasted_iota(jnp.int32, shape, 0)
        return lane == 0, lane == LANES - 1, row == 0, row == shape[0] - 1

    first_lane, last_lane, first_row, last_row = masks(tile)
    strip_first_lane, strip_last_lane, front, back = masks(strip)

    def chunk(j, carry):
        here = pl.ds(pl.multiple_of(j * LANES, LANES), LANES)
        left = pl.ds(pl.multiple_of(jnp.maximum(j - 1, 0) * LANES, LANES), LANES)
        right = pl.ds(pl.multiple_of(jnp.minimum(j + 1, chunks - 1) * LANES, LANES), LANES)

        def across(value, left_value, right_value, first, last):
            west = jnp.where(last & (j > 0), left_value, value)
            west = pltpu.roll(jnp.where(last & (j == 0), 0, west), 1, 1)
            east = jnp.where(first & (j < chunks - 1), right_value, value)
            east = pltpu.roll(jnp.where(first & (j == chunks - 1), 0, east), LANES - 1, 1)
            return (east - west).astype(jnp.float32)

        for r in range(tiles):
            rows = slice(r * SUBLANES, (r + 1) * SUBLANES)
            values = [volume_ref[0, s, rows, here] for s in range(slices)]
            remaining = jnp.ones(tile, jnp.float32)
            sums = [jnp.zeros(tile, jnp.float32) for _ in range(3)]
            for s in range(slices):
                value = values[s]
                up = volume_ref[0, s, (r - 1) * SUBLANES : r * SUBLANES, here] if r > 0 else value
                down = volume_ref[0, s, (r + 1) * SUBLANES : (r + 2) * SUBLANES, here] if r < tiles - 1 else value
                up = pltpu.roll(jnp.where(last_row, up, value), 1, 0)
                down = pltpu.roll(jnp.where(first_row, down, value), SUBLANES - 1, 0)
                grad_rows = (down - up).astype(jnp.float32)
                grad_cols = across(
                    value, volume_ref[0, s, rows, left], volume_ref[0, s, rows, right], first_lane, last_lane
                )
                squares = grad_rows * grad_rows + grad_cols * grad_cols
                facing = LIGHT_ROWS * grad_rows + LIGHT_COLS * grad_cols
                weight = remaining * opacity(volume_ref[1, s, rows, here], tile_alpha)
                remaining = remaining - weight
                if r == 0:
                    held_ref[0, s : s + 1, :] = weight[:1]
                    weight = jnp.where(first_row, 0.0, weight)
                if r == tiles - 1:
                    held_ref[1, s : s + 1, :] = weight[SUBLANES - 1 :]
                    weight = jnp.where(last_row, 0.0, weight)
                emitted = colors(value, tile_colors)
                if 0 < s < slices - 1:
                    grad_depth = (values[s + 1] - values[s - 1]).astype(jnp.float32)
                    weight = weight * shade(grad_depth, facing, squares)
                    for c in range(3):
                        sums[c] = sums[c] + emitted[c] * weight
                else:
                    end = int(s > 0)
                    face_ref[end, rows, here] = facing
                    square_ref[end, rows, here] = squares
                    weight = weight * (1.0 / 255.0)
                    for c in range(3):
                        lit_ref[end, c, rows, here] = emitted[c] * weight
            for c in range(3):
                base_ref[c, rows, here] = sums[c] * (1.0 / 255.0)
            base_ref[3, rows, here] = 1.0 - remaining

        for q, (edge, inner) in enumerate(((0, 1), (height - 1, height - 2))):
            value = volume_ref[0, :, edge, here]
            behind = pltpu.roll(jnp.where(back, 0, value), 1, 0)
            ahead = pltpu.roll(jnp.where(front, 0, value), slices - 1, 0)
            grad_ref[q, 0, :, here] = (ahead - behind).astype(jnp.float32)
            grad_ref[q, 1, :, here] = volume_ref[0, :, inner, here].astype(jnp.float32)
            grad_ref[q, 2, :, here] = across(
                value, volume_ref[0, :, edge, left], volume_ref[0, :, edge, right], strip_first_lane, strip_last_lane
            )
            weight = held_ref[q] * (1.0 / 255.0)
            emitted = colors(value, strip_colors)
            for c in range(3):
                strip_ref[q, c, :, here] = emitted[c] * weight
        return carry

    lax.fori_loop(0, chunks, chunk, 0)


def march_interior(volume, color_map, alpha_map, depth_count):
    _, slices, height, columns = volume.shape
    opacity_scale = OPACITY / (255.0 * slices * depth_count)
    shapes = [
        (4, height, columns),
        (2, height, columns),
        (2, height, columns),
        (2, 3, height, columns),
        (2, 3, slices, columns),
        (2, 3, slices, columns),
    ]
    voxels = slices * height * columns
    return pl.pallas_call(
        functools.partial(interior_kernel, opacity_scale),
        in_specs=[WHOLE] * 3,
        out_specs=[WHOLE] * len(shapes),
        out_shape=[jax.ShapeDtypeStruct(shape, jnp.float32) for shape in shapes],
        scratch_shapes=[pltpu.VMEM((2, slices, LANES), jnp.float32)],
        compiler_params=pltpu.CompilerParams(vmem_limit_bytes=24 * 1024 * 1024),
        cost_estimate=pl.CostEstimate(flops=voxels * 80, bytes_accessed=voxels * 20, transcendentals=voxels),
    )(volume, color_map, alpha_map.reshape(1, -1))


def edge_kernel(
    share, volume_ref, base_ref, face_ref, square_ref, lit_ref, grad_ref, strip_ref, rows_near_ref, rows_far_ref, far_ref, near_ref, out_ref
):
    _, slices, height, columns = volume_ref.shape
    tiles = height // SUBLANES
    tile = (SUBLANES, LANES)
    row = lax.broadcasted_iota(jnp.int32, tile, 0)
    first_row, last_row = row == 0, row == SUBLANES - 1
    level = lax.broadcasted_iota(jnp.int32, (slices, LANES), 0)
    front, back = level == 0, level == slices - 1
    odd, odd_row = parity("depth") == 1, parity("rows") == 1
    front_end, back_end = ends("depth")
    top_end, bottom_end = ends("rows")

    def chunk(j, carry):
        here = pl.ds(pl.multiple_of(j * LANES, LANES), LANES)
        rows_near = rows_near_ref[:, here].astype(jnp.float32)
        rows_far = rows_far_ref[:, here].astype(jnp.float32)
        above = jnp.where(top_end, 0.0, jnp.where(odd_row, rows_near, rows_far))
        below = jnp.where(bottom_end, 0.0, jnp.where(odd_row, rows_far, rows_near))
        far = far_ref[:, here].astype(jnp.float32)
        near = near_ref[:, here].astype(jnp.float32)
        before = jnp.where(front_end, 0.0, jnp.where(odd, near, far))
        after = jnp.where(back_end, 0.0, jnp.where(odd, far, near))
        extra = []
        for q, edge in enumerate((0, height - 1)):
            inner = grad_ref[q, 1, :, here]
            grad_rows = below - inner if q else inner - above
            grad_cols = grad_ref[q, 2, :, here]
            grad_depth = grad_ref[q, 0, :, here] + jnp.where(
                back, after[edge : edge + 1], jnp.where(front, -before[edge : edge + 1], 0.0)
            )
            shading = shade(
                grad_depth,
                LIGHT_ROWS * grad_rows + LIGHT_COLS * grad_cols,
                grad_rows * grad_rows + grad_cols * grad_cols,
            )
            extra.append([jnp.sum(strip_ref[q, c, :, here] * shading, axis=0, keepdims=True) for c in range(3)])
        for r in range(tiles):
            rows = slice(r * SUBLANES, (r + 1) * SUBLANES)
            planes = [base_ref[c, rows, here] for c in range(4)]
            for end in range(2):
                if end:
                    grad_depth = after[rows] - volume_ref[0, slices - 2, rows, here].astype(jnp.float32)
                else:
                    grad_depth = volume_ref[0, 1, rows, here].astype(jnp.float32) - before[rows]
                shading = shade(grad_depth, face_ref[end, rows, here], square_ref[end, rows, here])
                for c in range(3):
                    planes[c] = planes[c] + lit_ref[end, c, rows, here] * shading
            for c in range(3):
                if r == 0:
                    planes[c] = planes[c] + jnp.where(first_row, extra[0][c], 0.0)
                if r == tiles - 1:
                    planes[c] = planes[c] + jnp.where(last_row, extra[1][c], 0.0)
            for first in range(0, SUBLANES, share):
                block = jnp.concatenate([plane[first : first + share] for plane in planes], axis=0)
                out_ref[(r * SUBLANES + first) // share, :, here] = block.astype(jnp.bfloat16)
        return carry

    lax.fori_loop(0, columns // LANES, chunk, 0)


def add_edges(volume, interior, halos, depth_count):
    _, slices, height, columns = volume.shape
    share = height // depth_count
    return pl.pallas_call(
        functools.partial(edge_kernel, share),
        in_specs=[WHOLE] * 11,
        out_specs=WHOLE,
        out_shape=jax.ShapeDtypeStruct((depth_count, 4 * share, columns), jnp.bfloat16),
        compiler_params=pltpu.CompilerParams(vmem_limit_bytes=24 * 1024 * 1024),
    )(volume, *interior, *halos)


def finish_kernel(parts_ref, out_ref):
    count = parts_ref.shape[0]
    _, share, columns = out_ref.shape
    remaining = jnp.ones((share, columns), jnp.float32)
    sums = [jnp.zeros((share, columns), jnp.float32) for _ in range(3)]
    for k in range(count):
        part = parts_ref[k].astype(jnp.float32)
        for c in range(3):
            sums[c] = sums[c] + remaining * part[c * share : (c + 1) * share]
        remaining = remaining - remaining * part[3 * share :]
    for c in range(3):
        out_ref[c] = sums[c]
    out_ref[3] = 1.0 - remaining


def finish(parts, share):
    columns = parts.shape[2]
    return pl.pallas_call(
        finish_kernel,
        in_specs=[WHOLE],
        out_specs=WHOLE,
        out_shape=jax.ShapeDtypeStruct((4, share, columns), jnp.float32),
    )(parts)


def swapped(values, axis, start):
    size = lax.axis_size(axis)
    partner = list(range(size))
    for i in range(start, size - 1, 2):
        partner[i], partner[i + 1] = i + 1, i
    return lax.ppermute(values, axis, list(enumerate(partner)))


def body(volume, color_map, alpha_map):
    depth_count = lax.axis_size("depth")
    share = volume.shape[2] // depth_count
    rows_near, rows_far, far, near = cut_edges(volume)
    rows_far = swapped(rows_far, "rows", 1)
    rows_near = swapped(rows_near, "rows", 0)
    far = swapped(far, "depth", 1)
    near = swapped(near, "depth", 0)
    interior = march_interior(volume, color_map, alpha_map, depth_count)
    parts = add_edges(volume, interior, (rows_near, rows_far, far, near), depth_count)
    parts = lax.all_to_all(parts, "depth", 0, 0, tiled=True)
    return finish(parts, share)


def solution(mesh):
    in_specs = (P(None, "depth", "rows", None), P(), P())
    out_specs = P(None, ("rows", "depth"), None)
    return jax.shard_map(body, mesh=mesh, in_specs=in_specs, out_specs=out_specs, check_vma=False)
```

profile of v0, /device:TPU:8, one launch (start us, length us, event | category | flops | bytes accessed | tf_op | source)
XLA Modules:
  0.0 26.2 jit_solution(6401957686654204236)
XLA Ops:
  0.0 0.0 copy-start
  0.0 0.0 copy-start.2
  0.0 0.0 copy-start.1
  0.0 2.0 %shard_map.38 = (bf16[8,1024]{1,0:T(8,128)(2,1)}, bf16[8,1024]{1,0:T(8,128)(2,1)}, bf16[32,1024]{1,0:T(8,128)(2,1)}, bf16[32,1024]{1,0:T(8,128)(2,1)}) custom-call(s32[2,8,32,1024]{3,2,1,0:T(8,128)} %volume_ref.5), custom_call_target="tpu_custom_call" | custom-call | tf_op jit(solution)/shard_map/pallas_call | solution.py:64
  2.0 1.5 %collective-permute-start.2 = (bf16[32,1024]{1,0:T(8,128)(2,1)}, bf16[32,1024]{1,0:T(8,128)(2,1)S(1)}, u32[]{:S(2)}, u32[]{:S(2)}) collective-permute-start(bf16[32,1024]{1,0:T(8,128)(2,1)} %get-tuple-element.23), channel_id=1, source_target_pairs={{0,0},{4,8},{8,4},{12,16},{16,12},{20,24},{24,20},{28,28},{1,1},{5... | collective-permute-start | bytes 196616 | tf_op jit(solution)/shard_map/ppermute | solution.py:323
  3.5 2.1 %collective-permute-start.3 = (bf16[32,1024]{1,0:T(8,128)(2,1)}, bf16[32,1024]{1,0:T(8,128)(2,1)S(1)}, u32[]{:S(2)}, u32[]{:S(2)}) collective-permute-start(bf16[32,1024]{1,0:T(8,128)(2,1)} %get-tuple-element.24), channel_id=1, source_target_pairs={{0,4},{4,0},{8,12},{12,8},{16,20},{20,16},{24,28},{28,24},{1,5},{5... | collective-permute-start | bytes 196616 | tf_op jit(solution)/shard_map/ppermute | solution.py:323
  5.6 0.4 %collective-permute-start = (bf16[8,1024]{1,0:T(8,128)(2,1)}, bf16[8,1024]{1,0:T(8,128)(2,1)S(1)}, u32[]{:S(2)}, u32[]{:S(2)}) collective-permute-start(bf16[8,1024]{1,0:T(8,128)(2,1)} %get-tuple-element.21), channel_id=1, source_target_pairs={{0,1},{1,0},{2,3},{3,2},{4,5},{5,4},{6,7},{7,6},{8,9},{9,8},{10,11... | collective-permute-start | bytes 49160 | tf_op jit(solution)/shard_map/ppermute | solution.py:323
  6.0 4.6 %collective-permute-start.1 = (bf16[8,1024]{1,0:T(8,128)(2,1)}, bf16[8,1024]{1,0:T(8,128)(2,1)S(1)}, u32[]{:S(2)}, u32[]{:S(2)}) collective-permute-start(bf16[8,1024]{1,0:T(8,128)(2,1)} %get-tuple-element.22), channel_id=1, source_target_pairs={{0,0},{1,2},{2,1},{3,3},{4,4},{5,6},{6,5},{7,7},{8,8},{9,10},{10,9... | collective-permute-start | bytes 49160 | tf_op jit(solution)/shard_map/ppermute | solution.py:323
  10.6 0.0 copy-done
  10.6 0.0 copy-done.2
  10.6 0.0 copy-done.1
  10.7 3.3 %shard_map.37 = (f32[4,32,1024]{2,1,0:T(8,128)S(1)}, f32[2,32,1024]{2,1,0:T(8,128)S(1)}, f32[2,32,1024]{2,1,0:T(8,128)S(1)}, f32[2,3,32,1024]{3,2,1,0:T(8,128)S(...) custom-call(s32[2,8,32,1024]{3,2,1,0:T(8,128)S(1)} %copy-done, s32[3,256]{1,0:T(4,128)S(1)} %copy-done.1, ...), custom_call_target="tpu_custom_call" | custom-call | flops 20971520 | bytes 5242880 | tf_op jit(solution)/shard_map/pallas_call | solution.py:208
  14.0 0.0 collective-permute-done.rows_near_ref
  14.0 0.0 collective-permute-done.1.rows_far_ref
  14.0 0.0 collective-permute-done.2.far_ref
  14.0 0.0 collective-permute-done.3.near_ref
  14.0 0.5 %shard_map.39 = bf16[8,16,1024]{2,1,0:T(8,128)(2,1)S(1)} custom-call(s32[2,8,32,1024]{3,2,1,0:T(8,128)S(1)} %copy-done, f32[4,32,1024]{2,1,0:T(8,128)S(1)} %get-tuple-element.15.base_ref, f32[2,32,1024]{2,1,0:T(8,128)S(1)} %get-tuple-element.16.face_ref, f32[2,32,1024]{2,1,0:T(8,128)S(1)} %get-tuple-element.17.square_ref, ...), custom_call_target="tpu_custom_call" | custom-call | tf_op jit(solution)/shard_map/pallas_call | solution.py:284
  14.5 10.0 %all_to_all.5.parts_ref = bf16[8,16,1024]{2,1,0:T(8,128)(2,1)} all-to-all(bf16[8,16,1024]{2,1,0:T(8,128)(2,1)S(1)} %shard_map.39), channel_id=1, replica_groups=mesh['depth'=8,'rows'=4] {'depth'}, dimensions={0} | all-to-all | bytes 524288 | tf_op jit(solution)/shard_map/all_to_all | solution.py:336
  24.5 1.7 %shard_map.40 = f32[4,4,1024]{2,1,0:T(4,128)} custom-call(bf16[8,16,1024]{2,1,0:T(8,128)(2,1)} %all_to_all.5.parts_ref), custom_call_target="tpu_custom_call" | custom-call | tf_op jit(solution)/shard_map/pallas_call | solution.py:310
Async XLA Ops:
  0.0 10.6 %copy-start = (s32[2,8,32,1024]{3,2,1,0:T(8,128)S(1)}, s32[2,8,32,1024]{3,2,1,0:T(8,128)}, u32[]{:S(2)}) copy-start(s32[2,8,32,1024]{3,2,1,0:T(8,128)} %volume_ref.5) | copy-start | bytes 6291460
  0.0 10.6 %copy-start.2 = (s32[256]{0:T(256)S(1)}, s32[256]{0:T(256)}, u32[]{:S(2)}) copy-start(s32[256]{0:T(256)} %param.5) | copy-start | bytes 3076
  0.0 10.6 %copy-start.1 = (s32[3,256]{1,0:T(4,128)S(1)}, s32[3,256]{1,0:T(4,128)}, u32[]{:S(2)}) copy-start(s32[3,256]{1,0:T(4,128)} %color_ref.1) | copy-start | bytes 9220
  2.0 12.0 %collective-permute-start.2 = (bf16[32,1024]{1,0:T(8,128)(2,1)}, bf16[32,1024]{1,0:T(8,128)(2,1)S(1)}, u32[]{:S(2)}, u32[]{:S(2)}) collective-permute-start(bf16[32,1024]{1,0:T(8,128)(2,1)} %get-tuple-element.23), channel_id=1, source_target_pairs={{0,0},{4,8},{8,4},{12,16},{16,12},{20,24},{24,20},{28,28},{1,1},{5... | collective-permute-start | bytes 196616 | tf_op jit(solution)/shard_map/ppermute | solution.py:323
  3.5 10.5 %collective-permute-start.3 = (bf16[32,1024]{1,0:T(8,128)(2,1)}, bf16[32,1024]{1,0:T(8,128)(2,1)S(1)}, u32[]{:S(2)}, u32[]{:S(2)}) collective-permute-start(bf16[32,1024]{1,0:T(8,128)(2,1)} %get-tuple-element.24), channel_id=1, source_target_pairs={{0,4},{4,0},{8,12},{12,8},{16,20},{20,16},{24,28},{28,24},{1,5},{5... | collective-permute-start | bytes 196616 | tf_op jit(solution)/shard_map/ppermute | solution.py:323
  5.6 8.4 %collective-permute-start = (bf16[8,1024]{1,0:T(8,128)(2,1)}, bf16[8,1024]{1,0:T(8,128)(2,1)S(1)}, u32[]{:S(2)}, u32[]{:S(2)}) collective-permute-start(bf16[8,1024]{1,0:T(8,128)(2,1)} %get-tuple-element.21), channel_id=1, source_target_pairs={{0,1},{1,0},{2,3},{3,2},{4,5},{5,4},{6,7},{7,6},{8,9},{9,8},{10,11... | collective-permute-start | bytes 49160 | tf_op jit(solution)/shard_map/ppermute | solution.py:323
  6.0 8.0 %collective-permute-start.1 = (bf16[8,1024]{1,0:T(8,128)(2,1)}, bf16[8,1024]{1,0:T(8,128)(2,1)S(1)}, u32[]{:S(2)}, u32[]{:S(2)}) collective-permute-start(bf16[8,1024]{1,0:T(8,128)(2,1)} %get-tuple-element.22), channel_id=1, source_target_pairs={{0,0},{1,2},{2,1},{3,3},{4,4},{5,6},{6,5},{7,7},{8,8},{9,10},{10,9... | collective-permute-start | bytes 49160 | tf_op jit(solution)/shard_map/ppermute | solution.py:323
where the time goes:
time: 26.6 us; the launch traced here: 26.2 us
  blocking collectives  10 us (38%)
  starting transfers between devices  8.64 us (32%)
  Pallas kernels  7.49 us (28%)
    all_to_all x1, blocking collectives, body(): parts = lax.all_to_all(parts, 'depth', 0, 0, tiled=True)  10 us
    ppermute x4, starting transfers between devices, swapped(): return lax.ppermute(values, axis, list(enumerate(partner)))  8.64 us
    pallas_call x1, Pallas kernels, march_interior(): pl.pallas_call(functools.partial(interior_kernel, opacity_scale), in_spec...  3.31 us
    pallas_call x1, Pallas kernels, cut_edges(): pl.pallas_call(edges_kernel, in_specs=[pl.BlockSpec(memory_space=pl.ANY)]...  1.96 us
    pallas_call x1, Pallas kernels, finish(): pl.pallas_call(finish_kernel, in_specs=[WHOLE], out_specs=WHOLE, out_shap...  1.71 us
  transfers between devices with their start and end apart: 4, of which 0 were waited for; matrix products, arithmetic and copies ran while one was open for 0% of the time, Pallas kernels for 13%

commit v1 on v0

--- a/solution.py
+++ b/solution.py
@@ -27,7 +27,7 @@
     return position == 0, position == lax.axis_size(axis) - 1
 
 
-def edges_kernel(volume_ref, rows_near_out, rows_far_out, far_out, near_out, strip_ref, plane_ref, sems):
+def edges_kernel(volume_ref, rows_far_out, rows_near_out, far_out, near_out, strip_ref, plane_ref, sems):
     _, slices, height, _ = volume_ref.shape
     odd, odd_row = parity("depth"), parity("rows")
     last_tile = height // SUBLANES - 1
@@ -217,7 +217,7 @@
 
 
 def edge_kernel(
-    share, volume_ref, base_ref, face_ref, square_ref, lit_ref, grad_ref, strip_ref, rows_near_ref, rows_far_ref, far_ref, near_ref, out_ref
+    share, volume_ref, base_ref, face_ref, square_ref, lit_ref, grad_ref, strip_ref, rows_far_ref, rows_near_ref, far_ref, near_ref, out_ref
 ):
     _, slices, height, columns = volume_ref.shape
     tiles = height // SUBLANES
@@ -317,22 +317,20 @@
 
 def swapped(values, axis, start):
     size = lax.axis_size(axis)
-    partner = list(range(size))
-    for i in range(start, size - 1, 2):
-        partner[i], partner[i + 1] = i + 1, i
-    return lax.ppermute(values, axis, list(enumerate(partner)))
+    pairs = [((i + start) % size, (i + 1 + start) % size) for i in range(0, size, 2)]
+    return lax.ppermute(values, axis, pairs + [(j, i) for i, j in pairs])
 
 
 def body(volume, color_map, alpha_map):
     depth_count = lax.axis_size("depth")
     share = volume.shape[2] // depth_count
-    rows_near, rows_far, far, near = cut_edges(volume)
+    rows_far, rows_near, far, near = cut_edges(volume)
     rows_far = swapped(rows_far, "rows", 1)
     rows_near = swapped(rows_near, "rows", 0)
     far = swapped(far, "depth", 1)
     near = swapped(near, "depth", 0)
     interior = march_interior(volume, color_map, alpha_map, depth_count)
-    parts = add_edges(volume, interior, (rows_near, rows_far, far, near), depth_count)
+    parts = add_edges(volume, interior, (rows_far, rows_near, far, near), depth_count)
     parts = lax.all_to_all(parts, "depth", 0, 0, tiled=True)
     return finish(parts, share)
 

time: 26.6 us -> 25.4 us (0.955)
  the two profiles are of different devices: /device:TPU:8 before, /device:TPU:0 now
where the time goes in v1:
time: 25.4 us; the launch traced here: 25.2 us
  blocking collectives  10 us (39%)
  Pallas kernels  7.47 us (29%)
  starting transfers between devices  7.02 us (28%)
  waiting for transfers between devices  0.61 us (2%)
    all_to_all x1, blocking collectives, body(): parts = lax.all_to_all(parts, 'depth', 0, 0, tiled=True)  10 us
    ppermute x4, starting transfers between devices, swapped(): return lax.ppermute(values, axis, pairs + [(j, i) for i, j in pairs])  7.02 us
    pallas_call x1, Pallas kernels, march_interior(): pl.pallas_call(functools.partial(interior_kernel, opacity_scale), in_spec...  3.31 us
    pallas_call x1, Pallas kernels, cut_edges(): pl.pallas_call(edges_kernel, in_specs=[pl.BlockSpec(memory_space=pl.ANY)]...  1.95 us
    pallas_call x1, Pallas kernels, finish(): pl.pallas_call(finish_kernel, in_specs=[WHOLE], out_specs=WHOLE, out_shap...  1.71 us
    ppermute x4, waiting for transfers between devices, swapped(): return lax.ppermute(values, axis, pairs + [(j, i) for i, j in pairs])  0.61 us
  transfers between devices with their start and end apart: 4, of which 1 were waited for; matrix products, arithmetic and copies ran while one was open for 0% of the time, Pallas kernels for 13%

profile of v1, /device:TPU:0, one launch (start us, length us, event | category | flops | bytes accessed | tf_op | source)
XLA Modules:
  0.0 25.2 jit_solution(16489076142030957332)
XLA Ops:
  0.0 0.0 copy-start
  0.0 0.0 copy-start.2
  0.0 0.0 copy-start.1
  0.0 1.9 %shard_map.38 = (bf16[8,1024]{1,0:T(8,128)(2,1)}, bf16[8,1024]{1,0:T(8,128)(2,1)}, bf16[32,1024]{1,0:T(8,128)(2,1)}, bf16[32,1024]{1,0:T(8,128)(2,1)}) custom-call(s32[2,8,32,1024]{3,2,1,0:T(8,128)} %volume_ref.5), custom_call_target="tpu_custom_call" | custom-call | tf_op jit(solution)/shard_map/pallas_call | solution.py:64
  2.0 3.4 %collective-permute-start.2 = (bf16[32,1024]{1,0:T(8,128)(2,1)}, bf16[32,1024]{1,0:T(8,128)(2,1)S(1)}, u32[]{:S(2)}, u32[]{:S(2)}) collective-permute-start(bf16[32,1024]{1,0:T(8,128)(2,1)} %get-tuple-element.23), channel_id=1, source_target_pairs={{4,8},{12,16},{20,24},{28,0},{8,4},{16,12},{24,20},{0,28},{5,9},{1... | collective-permute-start | bytes 196616 | tf_op jit(solution)/shard_map/ppermute | solution.py:321
  5.4 0.0 collective-permute-start.3
  5.4 3.6 %collective-permute-start = (bf16[8,1024]{1,0:T(8,128)(2,1)}, bf16[8,1024]{1,0:T(8,128)(2,1)S(1)}, u32[]{:S(2)}, u32[]{:S(2)}) collective-permute-start(bf16[8,1024]{1,0:T(8,128)(2,1)} %get-tuple-element.21), channel_id=1, source_target_pairs={{1,2},{3,0},{2,1},{0,3},{5,6},{7,4},{6,5},{4,7},{9,10},{11,8},{10,... | collective-permute-start | bytes 49160 | tf_op jit(solution)/shard_map/ppermute | solution.py:321
  9.0 0.0 collective-permute-start.1
  9.0 0.0 copy-done
  9.0 0.0 copy-done.2
  9.0 0.0 copy-done.1
  9.0 3.3 %shard_map.37 = (f32[4,32,1024]{2,1,0:T(8,128)S(1)}, f32[2,32,1024]{2,1,0:T(8,128)S(1)}, f32[2,32,1024]{2,1,0:T(8,128)S(1)}, f32[2,3,32,1024]{3,2,1,0:T(8,128)S(...) custom-call(s32[2,8,32,1024]{3,2,1,0:T(8,128)S(1)} %copy-done, s32[3,256]{1,0:T(4,128)S(1)} %copy-done.1, ...), custom_call_target="tpu_custom_call" | custom-call | flops 20971520 | bytes 5242880 | tf_op jit(solution)/shard_map/pallas_call | solution.py:208
  12.3 0.0 collective-permute-done.rows_far_ref
  12.3 0.6 %collective-permute-done.1.rows_near_ref = bf16[8,1024]{1,0:T(8,128)(2,1)S(1)} collective-permute-done((bf16[8,1024]{1,0:T(8,128)(2,1)}, bf16[8,1024]{1,0:T(8,128)(2,1)S(1)}, u32[]{:S(2)}, u32[]{:S(2)}) %collective-permute-start.1) | collective-permute-done | bytes 16416 | tf_op jit(solution)/shard_map/ppermute | solution.py:321
  12.9 0.0 collective-permute-done.2.far_ref
  12.9 0.0 collective-permute-done.3.near_ref
  12.9 0.5 %shard_map.39 = bf16[8,16,1024]{2,1,0:T(8,128)(2,1)S(1)} custom-call(s32[2,8,32,1024]{3,2,1,0:T(8,128)S(1)} %copy-done, f32[4,32,1024]{2,1,0:T(8,128)S(1)} %get-tuple-element.15.base_ref, f32[2,32,1024]{2,1,0:T(8,128)S(1)} %get-tuple-element.16.face_ref, f32[2,32,1024]{2,1,0:T(8,128)S(1)} %get-tuple-element.17.square_ref, ...), custom_call_target="tpu_custom_call" | custom-call | tf_op jit(solution)/shard_map/pallas_call | solution.py:284
  13.4 10.0 %all_to_all.5.parts_ref = bf16[8,16,1024]{2,1,0:T(8,128)(2,1)} all-to-all(bf16[8,16,1024]{2,1,0:T(8,128)(2,1)S(1)} %shard_map.39), channel_id=1, replica_groups=mesh['depth'=8,'rows'=4] {'depth'}, dimensions={0} | all-to-all | bytes 524288 | tf_op jit(solution)/shard_map/all_to_all | solution.py:334
  23.5 1.7 %shard_map.40 = f32[4,4,1024]{2,1,0:T(4,128)} custom-call(bf16[8,16,1024]{2,1,0:T(8,128)(2,1)} %all_to_all.5.parts_ref), custom_call_target="tpu_custom_call" | custom-call | tf_op jit(solution)/shard_map/pallas_call | solution.py:310
Async XLA Ops:
  0.0 9.0 %copy-start = (s32[2,8,32,1024]{3,2,1,0:T(8,128)S(1)}, s32[2,8,32,1024]{3,2,1,0:T(8,128)}, u32[]{:S(2)}) copy-start(s32[2,8,32,1024]{3,2,1,0:T(8,128)} %volume_ref.5) | copy-start | bytes 6291460
  0.0 9.0 %copy-start.2 = (s32[256]{0:T(256)S(1)}, s32[256]{0:T(256)}, u32[]{:S(2)}) copy-start(s32[256]{0:T(256)} %param.5) | copy-start | bytes 3076
  0.0 9.0 %copy-start.1 = (s32[3,256]{1,0:T(4,128)S(1)}, s32[3,256]{1,0:T(4,128)}, u32[]{:S(2)}) copy-start(s32[3,256]{1,0:T(4,128)} %color_ref.1) | copy-start | bytes 9220
  2.0 11.0 %collective-permute-start.2 = (bf16[32,1024]{1,0:T(8,128)(2,1)}, bf16[32,1024]{1,0:T(8,128)(2,1)S(1)}, u32[]{:S(2)}, u32[]{:S(2)}) collective-permute-start(bf16[32,1024]{1,0:T(8,128)(2,1)} %get-tuple-element.23), channel_id=1, source_target_pairs={{4,8},{12,16},{20,24},{28,0},{8,4},{16,12},{24,20},{0,28},{5,9},{1... | collective-permute-start | bytes 196616 | tf_op jit(solution)/shard_map/ppermute | solution.py:321
  5.4 7.6 %collective-permute-start.3 = (bf16[32,1024]{1,0:T(8,128)(2,1)}, bf16[32,1024]{1,0:T(8,128)(2,1)S(1)}, u32[]{:S(2)}, u32[]{:S(2)}) collective-permute-start(bf16[32,1024]{1,0:T(8,128)(2,1)} %get-tuple-element.24), channel_id=1, source_target_pairs={{0,4},{8,12},{16,20},{24,28},{4,0},{12,8},{20,16},{28,24},{1,5},{9... | collective-permute-start | bytes 196616 | tf_op jit(solution)/shard_map/ppermute | solution.py:321
  5.4 6.9 %collective-permute-start = (bf16[8,1024]{1,0:T(8,128)(2,1)}, bf16[8,1024]{1,0:T(8,128)(2,1)S(1)}, u32[]{:S(2)}, u32[]{:S(2)}) collective-permute-start(bf16[8,1024]{1,0:T(8,128)(2,1)} %get-tuple-element.21), channel_id=1, source_target_pairs={{1,2},{3,0},{2,1},{0,3},{5,6},{7,4},{6,5},{4,7},{9,10},{11,8},{10,... | collective-permute-start | bytes 49160 | tf_op jit(solution)/shard_map/ppermute | solution.py:321
  9.0 3.9 %collective-permute-start.1 = (bf16[8,1024]{1,0:T(8,128)(2,1)}, bf16[8,1024]{1,0:T(8,128)(2,1)S(1)}, u32[]{:S(2)}, u32[]{:S(2)}) collective-permute-start(bf16[8,1024]{1,0:T(8,128)(2,1)} %get-tuple-element.22), channel_id=1, source_target_pairs={{0,1},{2,3},{1,0},{3,2},{4,5},{6,7},{5,4},{7,6},{8,9},{10,11},{9,8... | collective-permute-start | bytes 49160 | tf_op jit(solution)/shard_map/ppermute | solution.py:321
